TPU v7x, 128 devices: a whole 4x4x4 slice. The times are simulated.
128 devices in a mesh: ctx: 16 (over x, y), wa: 8 (over z, core).
Axes of the slice: x: 4, y: 4, z: 4, core: 2. Of those that a mesh axis runs over, the one named last changes fastest.
Arguments:
- layer_input: bfloat16 [8, 2048, 896], P('wa', 'ctx'), may hold values from -6 to 6
- positions: int32 [8, 2048], P('wa', 'ctx'), may hold values from 0 to 2047, as said below
- attention_gain: bfloat16 [896], P('wa'), may hold values from 0.5 to 1.5
- projection: bfloat16 [896, 1152], P('wa'), may hold values from -0.1875 to 0.1875
- projection_biases: bfloat16 [1152], P('wa'), may hold values from -3 to 3
- output_matrix: bfloat16 [896, 896], P('wa'), may hold values from -3.5 to 3.5
- feed_gain: bfloat16 [896], P('wa'), may hold values from 0.5 to 1.5
- gate_up_matrix: bfloat16 [896, 9728], P('wa'), may hold values from -0.1875 to 0.1875
- down_matrix: bfloat16 [4864, 896], P('wa'), may hold values from -0.078125 to 0.078125
- cotangent: bfloat16 [8, 2048, 896], P('wa', 'ctx'), may hold values from -6 to 6
Outputs:
- layer_output: bfloat16 [8, 2048, 896], P('wa', 'ctx')
- input_grad: float32 [8, 2048, 896], P('wa', 'ctx')
- attention_gain_grad: float32 [896], P('wa')
- projection_grad: float32 [896, 1152], P('wa')
- projection_bias_grad: float32 [1152], P('wa')
- output_weight_grad: float32 [896, 896], P('wa')
- feed_gain_grad: float32 [896], P('wa')
- gate_up_grad: float32 [896, 9728], P('wa')
- down_grad: float32 [4864, 896], P('wa')
Inputs may be any that keep to these rules, and one draw needn't show every extreme that they name: `positions`: each sequence is a run of documents: the first token of a sequence has position 0, and every later token has position 0 (it opens a document) or one more than the token before. The first sequence is one document over all 2048 tokens.
All inputs are finite; a program needn't handle non-finite values.
Results may differ from a plain program's by a relative error of at most 0.024.
Values may be sent and summed in bfloat16 or wider, within the bound.
No kernel may reach another device: no remote copies, remote signals or barrier semaphores. Data moves between devices by JAX's collectives and lax.ppermute only.
A program may use at most 128 MiB of HBM per device.

v0:
```python
import math

import jax
import jax.numpy as jnp
from jax import lax
from jax.sharding import PartitionSpec as P

QUERY_HEADS = 14
KEY_VALUE_HEADS = 2
HEAD_SIZE = 64
FF = 4864


EPS = 1e-06
THETA = 1000000.0
NEG = -1e30


def rows_product(left, right):
    return lax.dot_general(
        left, right, (((0,), (0,)), ((), ())), preferred_element_type=jnp.float32
    )


def column_product(left, right):
    return lax.dot_general(
        left, right, (((1,), (1,)), ((), ())), preferred_element_type=jnp.float32
    )


def norm_rows(value, gain):
    return value * lax.rsqrt(jnp.mean(value * value, axis=-1, keepdims=True) + EPS) * gain


def rotate(tensor, cosine_table, sine_table):
    half = tensor.shape[-1] // 2
    first = tensor[..., :half]
    second = tensor[..., half:]
    return jnp.concatenate(
        [first * cosine_table - second * sine_table, second * cosine_table + first * sine_table],
        axis=-1,
    )


def inverse_rotate(tensor, cosine_table, sine_table):
    half = tensor.shape[-1] // 2
    first = tensor[..., :half]
    second = tensor[..., half:]
    return jnp.concatenate(
        [first * cosine_table + second * sine_table, second * cosine_table - first * sine_table],
        axis=-1,
    )


def angles(positions):
    half = HEAD_SIZE // 2
    inverse = THETA ** (-(jnp.arange(half) * 2.0 / HEAD_SIZE))
    turned = positions.astype(jnp.float32)[:, None] * inverse.astype(jnp.float32)
    return (jnp.cos(turned), jnp.sin(turned))


def swiglu(joined_heads):
    return jax.nn.silu(joined_heads[:, :FF]) * joined_heads[:, FF:]


def block_scores(grouped_queries, key_rows, block_start, query_index, query_pos):
    block_count = key_rows.shape[0]
    raw = jnp.einsum(
        "cmxz,omz->mxco",
        grouped_queries,
        key_rows.reshape(block_count, KEY_VALUE_HEADS, HEAD_SIZE),
        preferred_element_type=jnp.float32,
    ) * HEAD_SIZE ** (-0.5)
    gap = query_index[:, None] - (block_start + jnp.arange(block_count))[None, :]
    seen = (gap >= 0) & (gap <= query_pos[:, None])
    return (jnp.where(seen, raw, NEG), seen)


def keep_carry(carry):
    return carry


def key_stats(grouped_queries, key_rows, query_index, query_pos, token_block):
    array_shape = (KEY_VALUE_HEADS, QUERY_HEADS // KEY_VALUE_HEADS, grouped_queries.shape[0])

    def visit(which, carry):
        block_start = which * token_block

        def update(state):
            peak, total = state
            token_piece = lax.dynamic_slice_in_dim(key_rows, block_start, token_block, 0)
            masked, seen = block_scores(
                grouped_queries, token_piece, block_start, query_index, query_pos
            )
            raised = jnp.maximum(peak, jnp.max(masked, axis=-1))
            added = jnp.sum(jnp.where(seen, jnp.exp(masked - raised[..., None]), 0.0), axis=-1)
            return (raised, total * jnp.exp(peak - raised) + added)

        return lax.cond(block_start <= query_index[-1], update, keep_carry, carry)

    start_state = (jnp.full(array_shape, NEG, jnp.float32), jnp.zeros(array_shape, jnp.float32))
    return lax.fori_loop(0, key_rows.shape[0] // token_block, visit, start_state)


def key_mix(
    grouped_queries, key_rows, value_rows, query_index, query_pos, peak, total, token_block
):
    array_shape = (
        grouped_queries.shape[0],
        KEY_VALUE_HEADS,
        QUERY_HEADS // KEY_VALUE_HEADS,
        HEAD_SIZE,
    )

    def visit(which, carry):
        block_start = which * token_block

        def update(mixed):
            token_piece = lax.dynamic_slice_in_dim(key_rows, block_start, token_block, 0)
            value_segment = lax.dynamic_slice_in_dim(
                value_rows, block_start, token_block, 0
            ).reshape(token_block, KEY_VALUE_HEADS, HEAD_SIZE)
            masked, seen = block_scores(
                grouped_queries, token_piece, block_start, query_index, query_pos
            )
            probs = jnp.where(seen, jnp.exp(masked - peak[..., None]) / total[..., None], 0.0)
            return mixed + jnp.einsum(
                "kgts,skd->tkgd",
                probs.astype(jnp.bfloat16),
                value_segment,
                preferred_element_type=jnp.float32,
            )

        return lax.cond(block_start <= query_index[-1], update, keep_carry, carry)

    return lax.fori_loop(
        0, key_rows.shape[0] // token_block, visit, jnp.zeros(array_shape, jnp.float32)
    )


def key_grads(
    grouped_queries,
    key_rows,
    value_rows,
    mix_grad,
    delta,
    query_index,
    query_pos,
    peak,
    total,
    token_block,
):
    length = key_rows.shape[0]
    model_width = KEY_VALUE_HEADS * HEAD_SIZE

    def visit(which, carry):
        block_start = which * token_block

        def update(state):
            query_grad, key_grad, value_grad = state
            token_piece = lax.dynamic_slice_in_dim(key_rows, block_start, token_block, 0)
            value_segment = lax.dynamic_slice_in_dim(
                value_rows, block_start, token_block, 0
            ).reshape(token_block, KEY_VALUE_HEADS, HEAD_SIZE)
            masked, seen = block_scores(
                grouped_queries, token_piece, block_start, query_index, query_pos
            )
            probs = jnp.where(seen, jnp.exp(masked - peak[..., None]) / total[..., None], 0.0)
            prob_grad = jnp.einsum(
                "cmxz,omz->mxco", mix_grad, value_segment, preferred_element_type=jnp.float32
            )
            score_grad = (probs * (prob_grad - delta[..., None])).astype(jnp.bfloat16)
            query_grad = query_grad + jnp.einsum(
                "kgts,skd->tkgd",
                score_grad,
                token_piece.reshape(token_block, KEY_VALUE_HEADS, HEAD_SIZE),
                preferred_element_type=jnp.float32,
            )
            key_part = jnp.einsum(
                "kgts,tkgd->skd", score_grad, grouped_queries, preferred_element_type=jnp.float32
            ).reshape(token_block, model_width)
            value_part = jnp.einsum(
                "kgts,tkgd->skd",
                probs.astype(jnp.bfloat16),
                mix_grad,
                preferred_element_type=jnp.float32,
            ).reshape(token_block, model_width)
            key_grad = lax.dynamic_update_slice_in_dim(key_grad, key_part, block_start, 0)
            value_grad = lax.dynamic_update_slice_in_dim(value_grad, value_part, block_start, 0)
            return (query_grad, key_grad, value_grad)

        return lax.cond(block_start <= query_index[-1], update, keep_carry, carry)

    start_state = (
        jnp.zeros(grouped_queries.shape, jnp.float32),
        jnp.zeros((length, model_width), jnp.float32),
        jnp.zeros((length, model_width), jnp.float32),
    )
    return lax.fori_loop(0, length // token_block, visit, start_state)


def on_device(
    layer_input,
    positions,
    attention_gain,
    projection,
    projection_biases,
    output_matrix,
    feed_gain,
    gate_up_matrix,
    down_matrix,
    cotangent,
):
    shards = (
        attention_gain,
        projection,
        projection_biases,
        output_matrix,
        feed_gain,
        gate_up_matrix,
        down_matrix,
    )
    gain_one, full_proj, full_bias, complete_output, gain_two, full_gate_up, full_down = (
        lax.all_gather(shards[0], "wa", axis=0, tiled=True),
        lax.all_gather(shards[1], "wa", axis=0, tiled=True),
        lax.all_gather(shards[2], "wa", axis=0, tiled=True),
        lax.all_gather(shards[3], "wa", axis=0, tiled=True),
        lax.all_gather(shards[4], "wa", axis=0, tiled=True),
        lax.all_gather(shards[5], "wa", axis=0, tiled=True),
        lax.all_gather(shards[6], "wa", axis=0, tiled=True),
    )
    block_count = layer_input.shape[1]
    head_group = QUERY_HEADS // KEY_VALUE_HEADS
    query_total_width = QUERY_HEADS * HEAD_SIZE
    key_total_width = KEY_VALUE_HEADS * HEAD_SIZE
    decoder_layer = layer_input[0].astype(jnp.float32)
    query_pos = positions[0]
    query_index = lax.axis_index("ctx") * block_count + jnp.arange(block_count, dtype=jnp.int32)
    first_normed = norm_rows(decoder_layer, gain_one.astype(jnp.float32)).astype(jnp.bfloat16)
    projected_rows = jnp.dot(
        first_normed, full_proj, preferred_element_type=jnp.float32
    ) + full_bias.astype(jnp.float32)
    cosine_table, sine_table = angles(query_pos)
    cosine_table = cosine_table[:, None, :]
    sine_table = sine_table[:, None, :]
    query_rows = rotate(
        projected_rows[:, :query_total_width].reshape(block_count, QUERY_HEADS, HEAD_SIZE),
        cosine_table,
        sine_table,
    ).astype(jnp.bfloat16)
    key_rows = rotate(
        projected_rows[:, query_total_width : query_total_width + key_total_width].reshape(
            block_count, KEY_VALUE_HEADS, HEAD_SIZE
        ),
        cosine_table,
        sine_table,
    )
    key_rows = key_rows.astype(jnp.bfloat16).reshape(block_count, key_total_width)
    value_rows = projected_rows[:, query_total_width + key_total_width :].astype(jnp.bfloat16)
    all_keys, all_values = (
        lax.all_gather(key_rows, "ctx", axis=0, tiled=True),
        lax.all_gather(value_rows, "ctx", axis=0, tiled=True),
    )
    token_block = math.gcd(512, all_keys.shape[0])
    grouped_queries = query_rows.reshape(block_count, KEY_VALUE_HEADS, head_group, HEAD_SIZE)
    peak, total = key_stats(grouped_queries, all_keys, query_index, query_pos, token_block)
    mixed = key_mix(
        grouped_queries, all_keys, all_values, query_index, query_pos, peak, total, token_block
    )
    attention_output = mixed.reshape(block_count, query_total_width).astype(jnp.bfloat16)
    middle_state = decoder_layer + jnp.dot(
        attention_output, complete_output, preferred_element_type=jnp.float32
    )
    second_normed = norm_rows(middle_state, gain_two.astype(jnp.float32)).astype(jnp.bfloat16)
    joined_heads = jnp.dot(second_normed, full_gate_up, preferred_element_type=jnp.float32)
    hidden_f, swiglu_pull = jax.vjp(swiglu, joined_heads)
    hidden_state = hidden_f.astype(jnp.bfloat16)
    result = (
        middle_state + jnp.dot(hidden_state, full_down, preferred_element_type=jnp.float32)
    ).astype(jnp.bfloat16)
    gain_one, full_proj, full_bias, complete_output, gain_two, full_gate_up, full_down = (
        lax.all_gather(shards[0], "wa", axis=0, tiled=True),
        lax.all_gather(shards[1], "wa", axis=0, tiled=True),
        lax.all_gather(shards[2], "wa", axis=0, tiled=True),
        lax.all_gather(shards[3], "wa", axis=0, tiled=True),
        lax.all_gather(shards[4], "wa", axis=0, tiled=True),
        lax.all_gather(shards[5], "wa", axis=0, tiled=True),
        lax.all_gather(shards[6], "wa", axis=0, tiled=True),
    )
    out_grad = cotangent[0]
    down_local = rows_product(hidden_state, out_grad)
    hidden_grad = column_product(out_grad, full_down)
    joined_grad = swiglu_pull(hidden_grad)[0].astype(jnp.bfloat16)
    gate_up_local = rows_product(second_normed, joined_grad)
    normed_two_grad = column_product(joined_grad, full_gate_up)
    _, norm_two_pull = jax.vjp(norm_rows, middle_state, gain_two.astype(jnp.float32))
    middle_part, gain_two_local = norm_two_pull(normed_two_grad)
    middle_grad = out_grad.astype(jnp.float32) + middle_part
    middle_lower = middle_grad.astype(jnp.bfloat16)
    out_weight_local = rows_product(attention_output, middle_lower)
    mix_grad = (
        column_product(middle_lower, complete_output)
        .astype(jnp.bfloat16)
        .reshape(block_count, KEY_VALUE_HEADS, head_group, HEAD_SIZE)
    )
    delta = jnp.einsum("tkgd,tkgd->kgt", mix_grad.astype(jnp.float32), mixed)
    query_grad, key_grad, value_grad = key_grads(
        grouped_queries,
        all_keys,
        all_values,
        mix_grad,
        delta,
        query_index,
        query_pos,
        peak,
        total,
        token_block,
    )
    local_key_rows, own_values = (
        lax.psum_scatter(
            key_grad.astype(jnp.bfloat16), "ctx", scatter_dimension=0, tiled=True
        ).astype(jnp.float32),
        lax.psum_scatter(
            value_grad.astype(jnp.bfloat16), "ctx", scatter_dimension=0, tiled=True
        ).astype(jnp.float32),
    )
    score_scale = HEAD_SIZE ** (-0.5)
    query_back = inverse_rotate(
        (query_grad * score_scale).reshape(block_count, QUERY_HEADS, HEAD_SIZE),
        cosine_table,
        sine_table,
    ).reshape(block_count, query_total_width)
    key_restored = inverse_rotate(
        (local_key_rows * score_scale).reshape(block_count, KEY_VALUE_HEADS, HEAD_SIZE),
        cosine_table,
        sine_table,
    ).reshape(block_count, key_total_width)
    projected_grad = jnp.concatenate([query_back, key_restored, own_values], axis=1).astype(
        jnp.bfloat16
    )
    proj_local = rows_product(first_normed, projected_grad)
    bias_local = jnp.sum(projected_grad.astype(jnp.float32), axis=0)
    normed_one_grad = column_product(projected_grad, full_proj)
    _, norm_one_pull = jax.vjp(norm_rows, decoder_layer, gain_one.astype(jnp.float32))
    layer_part, gain_one_local = norm_one_pull(normed_one_grad)
    input_grad = middle_grad + layer_part
    local_all = (
        gain_one_local,
        proj_local,
        bias_local,
        out_weight_local,
        gain_two_local,
        gate_up_local,
        down_local,
    )
    rows_all = (
        lax.psum_scatter(
            local_all[0].astype(jnp.bfloat16), "wa", scatter_dimension=0, tiled=True
        ).astype(jnp.float32),
        lax.psum_scatter(
            local_all[1].astype(jnp.bfloat16), "wa", scatter_dimension=0, tiled=True
        ).astype(jnp.float32),
        lax.psum_scatter(
            local_all[2].astype(jnp.bfloat16), "wa", scatter_dimension=0, tiled=True
        ).astype(jnp.float32),
        lax.psum_scatter(
            local_all[3].astype(jnp.bfloat16), "wa", scatter_dimension=0, tiled=True
        ).astype(jnp.float32),
        lax.psum_scatter(
            local_all[4].astype(jnp.bfloat16), "wa", scatter_dimension=0, tiled=True
        ).astype(jnp.float32),
        lax.psum_scatter(
            local_all[5].astype(jnp.bfloat16), "wa", scatter_dimension=0, tiled=True
        ).astype(jnp.float32),
        lax.psum_scatter(
            local_all[6].astype(jnp.bfloat16), "wa", scatter_dimension=0, tiled=True
        ).astype(jnp.float32),
    )
    totals = (
        lax.psum(rows_all[0].astype(jnp.bfloat16), "ctx").astype(jnp.float32),
        lax.psum(rows_all[1].astype(jnp.bfloat16), "ctx").astype(jnp.float32),
        lax.psum(rows_all[2].astype(jnp.bfloat16), "ctx").astype(jnp.float32),
        lax.psum(rows_all[3].astype(jnp.bfloat16), "ctx").astype(jnp.float32),
        lax.psum(rows_all[4].astype(jnp.bfloat16), "ctx").astype(jnp.float32),
        lax.psum(rows_all[5].astype(jnp.bfloat16), "ctx").astype(jnp.float32),
        lax.psum(rows_all[6].astype(jnp.bfloat16), "ctx").astype(jnp.float32),
    )
    return (
        result[None],
        input_grad[None],
        totals[0],
        totals[1],
        totals[2],
        totals[3],
        totals[4],
        totals[5],
        totals[6],
    )


def solution(mesh):
    placed = (
        P("wa", "ctx", None),
        P("wa", "ctx"),
        P("wa"),
        P("wa", None),
        P("wa"),
        P("wa", None),
        P("wa"),
        P("wa", None),
        P("wa", None),
        P("wa", "ctx", None),
    )
    return jax.shard_map(
        on_device,
        mesh=mesh,
        in_specs=placed,
        out_specs=(
            P("wa", "ctx", None),
            P("wa", "ctx", None),
            P("wa"),
            P("wa", None),
            P("wa"),
            P("wa", None),
            P("wa"),
            P("wa", None),
            P("wa", None),
        ),
        check_vma=False,
    )
```

profile of v0, /device:TPU:1, one launch (start us, length us, event | category | flops | bytes accessed | tf_op | source)
XLA Modules:
  0.0 754.6 jit_solution(8235953006526993133)
XLA Ops:
  12.7 14.7 %all-reduce.11 = (bf16[1152]{0:T(1024)(128)(2,1)S(1)}, bf16[896]{0:T(1024)(128)(2,1)S(1)}, bf16[896]{0:T(1024)(128)(2,1)S(1)}) all-reduce(bf16[1152]{0:T(1024)(128)(2,1)S(1)} %dynamic-update-slice.1, bf16[896]{0:T(1024)(128)(2,1)S(1)} %dynamic-update-slice, bf16[896]{0:T(1024)(128)(2,1)S(1)} %dynamic-update-slice.2), channel_id=1, replica_groups=mesh['ctx'=16,'wa'=8] {'wa'}, use_global_device_ids=true, to_apply=%add.3 | all-reduce | flops 2944 | bytes 11776
  27.8 11.0 %all-gather.5.cloned.1.call-done = bf16[896,1152]{1,0:T(8,128)(2,1)} async-done(((bf16[112,1152]{1,0:T(8,128)(2,1)}), bf16[896,1152]{1,0:T(8,128)(2,1)}) %all-gather.5.cloned.1.call-update) | async-done | bytes 2064400 | tf_op jit(solution)/shard_map/all_gather | solution.py:225
  38.8 2.1 convolution_add_fusion
  41.0 19.7 %all_gather.36 = bf16[2048,128]{1,0:T(8,128)(2,1)S(1)} all-gather(bf16[128,128]{1,0:T(8,128)(2,1)S(1)} %slice.112), channel_id=1, replica_groups=mesh['ctx'=16,'wa'=8] {'ctx'}, dimensions={0}, use_global_device_ids=true | all-gather | bytes 557056 | tf_op jit(solution)/shard_map/all_gather | solution.py:262
  61.3 18.5 %all_gather.37 = bf16[2048,128]{0,1:T(8,128)(2,1)S(1)} all-gather(bf16[128,128]{0,1:T(8,128)(2,1)S(1)} %bitcast.193), channel_id=1, replica_groups=mesh['ctx'=16,'wa'=8] {'ctx'}, dimensions={0}, use_global_device_ids=true | all-gather | bytes 557056 | tf_op jit(solution)/shard_map/all_gather | solution.py:261
  79.9 6.9 while.48
  81.1 1.8 conditional.6
  82.0 0.9 select_reduce_fusion
  86.8 6.8 while.49
  88.1 1.6 conditional.7
  88.3 1.4 fusion.9
  94.5 2.1 multiply_reduce_fusion.2
  96.6 58.3 %all-gather.9.cloned.1.call-done = bf16[896,9728]{1,0:T(8,128)(2,1)} async-done(((bf16[112,9728]{1,0:T(8,128)(2,1)}), bf16[896,9728]{1,0:T(8,128)(2,1)}) %all-gather.9.cloned.1.call-update) | async-done | bytes 17432592 | tf_op jit(solution)/shard_map/all_gather | solution.py:229
  154.9 11.1 %fusion.52 = f32[128,9728]{1,0:T(8,128)} fusion(bf16[896,9728]{1,0:T(8,128)(2,1)} %all-gather.9.cloned.1.call-done, f32[128,896]{1,0:T(8,128)S(1)} %get-tuple-element.793, f32[896]{0:T(1024)S(1)} %convert_element_type.180, f32[128]{0:T(128)S(1)} %fusion.49), kind=kOutput, calls=%fused_computation.121 | convolution fusion | flops 2231713792 | bytes 22876160 | tf_op jit(solution)/shard_map/dot_general | solution.py:275
  166.0 42.3 %all-gather.11.cloned.1.call-done = bf16[4864,896]{1,0:T(8,128)(2,1)} async-done(((bf16[608,896]{1,0:T(8,128)(2,1)}), bf16[4864,896]{1,0:T(8,128)(2,1)}) %all-gather.11.cloned.1.call-update) | async-done | bytes 8716304 | tf_op jit(solution)/shard_map/all_gather | solution.py:230
  208.3 8.9 %fusion.40 = (f32[128,4864]{1,0:T(8,128)S(1)}, f32[128,4864]{1,0:T(8,128)}, bf16[128,4864]{1,0:T(8,128)(2,1)S(1)}) fusion(f32[128,9728]{1,0:T(8,128)} %fusion.52, bf16[4864,896]{1,0:T(8,128)(2,1)} %all-gather.11.cloned.1.call-done, bf16[1,128,896]{2,1,0:T(8,128)(2,1)} %param.31), kind=kOutput, calls=%fused_computation.87 | convolution fusion | flops 1124401152 | bytes 20152320 | tf_op jit(solution)/shard_map/dot_general | solution.py:26
  217.2 13.9 %multiply_reduce_fusion = (bf16[896]{0:T(1024)(128)(2,1)S(1)}, f32[128]{0:T(128)S(1)}, f32[128,896]{1,0:T(8,128)}) fusion(f32[128,896]{1,0:T(8,128)S(1)} %get-tuple-element.793, f32[128]{0:T(128)S(1)} %fusion.49, f32[896]{0:T(1024)S(1)} %convert_element_type.180, bf16[896,9728]{1,0:T(8,128)(2,1)} %all-gather.9.cloned.1.call-done, ...), kind=kOutput, calls=%fused_computation.81 | convolution fusion | flops 2234547200 | bytes 23337216 | tf_op jit(solution)/shard_map/dot_general | solution.py:26
  231.1 1.3 fusion.33
  233.2 2.0 convolution_convert_fusion.4
  236.4 0.9 broadcast.158.clone
  237.2 10.7 %while.50 = (s32[]{:T(128)}, f32[128,2,7,64]{0,3,2,1:T(8,128)S(1)}, bf16[2048,128]{0,1:T(8,128)(2,1)}, bf16[2048,128]{0,1:T(8,128)(2,1)}, s32[128]{0:T(128)S(1)}...) while((s32[]{:T(128)}, f32[128,2,7,64]{0,3,2,1:T(8,128)S(1)}, ...), condition=%wide.region_16.17_spmd, body=%wide.region_13.16_spmd.sunk | while | flops 595837440 | bytes 20212104 | solution.py:199
  238.4 5.6 conditional.8
  238.6 1.2 fusion.19
  239.8 0.9 constant_dynamic-slice_fusion.3
  247.9 2.1 copy.74
  250.2 2.1 copy.72
  252.4 2.8 convolution_convert_fusion.3
  255.4 81.3 %reduce-scatter.21.cloned.1.call-done = bf16[128,128]{1,0:T(8,128)(2,1)} async-done(((bf16[2048,128]{1,0:T(8,128)(2,1)}), bf16[128,128]{1,0:T(8,128)(2,1)}) %reduce-scatter.21.cloned.1.call-update) | async-done | bytes 32784
  336.7 0.9 copy.75
  337.5 74.0 %reduce-scatter.19.cloned.1.call-done = bf16[128,128]{1,0:T(8,128)(2,1)} async-done(((bf16[2048,128]{1,0:T(8,128)(2,1)}), bf16[128,128]{1,0:T(8,128)(2,1)}) %reduce-scatter.19.cloned.1.call-update) | async-done | bytes 32784
  411.5 0.9 copy.73
  412.5 2.1 convolution_convert_fusion.2
  414.7 4.7 convolution_convert_fusion.1
  419.4 10.3 %convolution_convert_fusion = bf16[896,9728]{1,0:T(8,128)(2,1)} fusion(f32[128,4864]{1,0:T(8,128)} %get-tuple-element.778, f32[128,4864]{1,0:T(8,128)} %copy-done, f32[128,896]{1,0:T(8,128)S(1)} %get-tuple-element.793, f32[896]{0:T(1024)S(1)} %convert_element_type.180, f32[128]{0:T(128)S(1)} %fusion.49), kind=kOutput, calls=%fused_computation.47 | convolution fusion | flops 2242920448 | bytes 22876160 | tf_op jit(solution)/shard_map/dot_general | solution.py:20
  429.8 15.2 %reduce-scatter.13.cloned.1.call-done = bf16[112,896]{1,0:T(8,128)(2,1)} async-done(((bf16[896,896]{1,0:T(8,128)(2,1)}), bf16[112,896]{1,0:T(8,128)(2,1)}) %reduce-scatter.13.cloned.1.call-update) | async-done | bytes 200720 | tf_op jit(solution)/shard_map/reduce_scatter | solution.py:366
  445.0 35.4 %reduce-scatter.11.cloned.1.call-done = bf16[112,1152]{1,0:T(8,128)(2,1)} async-done(((bf16[896,1152]{1,0:T(8,128)(2,1)}), bf16[112,1152]{1,0:T(8,128)(2,1)}) %reduce-scatter.11.cloned.1.call-update) | async-done | bytes 258064 | tf_op jit(solution)/shard_map/reduce_scatter | solution.py:360
  480.4 57.8 %reduce-scatter.17.cloned.1.call-done = bf16[608,896]{1,0:T(8,128)(2,1)} async-done(((bf16[4864,896]{1,0:T(8,128)(2,1)}), bf16[608,896]{1,0:T(8,128)(2,1)}) %reduce-scatter.17.cloned.1.call-update) | async-done | bytes 1089552 | tf_op jit(solution)/shard_map/reduce_scatter | solution.py:375
  538.1 97.0 %reduce-scatter.15.cloned.1.call-done = bf16[112,9728]{1,0:T(8,128)(2,1)} async-done(((bf16[896,9728]{1,0:T(8,128)(2,1)}), bf16[112,9728]{1,0:T(8,128)(2,1)}) %reduce-scatter.15.cloned.1.call-update) | async-done | bytes 2179088 | tf_op jit(solution)/shard_map/reduce_scatter | solution.py:372
  636.5 5.8 fusion.28
  642.4 0.9 fusion.32
  643.3 13.8 %all-reduce.10 = (bf16[896]{0:T(1024)(128)(2,1)S(1)}, bf16[1152]{0:T(1024)(128)(2,1)S(1)}, bf16[896]{0:T(1024)(128)(2,1)S(1)}) all-reduce(bf16[896]{0:T(1024)(128)(2,1)S(1)} %get-tuple-element.698, bf16[1152]{0:T(1024)(128)(2,1)S(1)} %fusion.53, bf16[896]{0:T(1024)(128)(2,1)S(1)} %get-tuple-element.696), channel_id=4, replica_groups=mesh['ctx'=16,'wa'=8] {'wa'}, use_global_device_ids=true, to_apply=%region_21.22.clone | all-reduce | flops 2944 | bytes 11776
  657.3 33.2 %all-reduce.8 = (bf16[112]{0:T(256)(128)(2,1)S(1)}, bf16[144]{0:T(256)(128)(2,1)S(1)}, bf16[112]{0:T(256)(128)(2,1)S(1)}) all-reduce(bf16[112]{0:T(256)(128)(2,1)S(1)} %dynamic-slice.4, bf16[144]{0:T(256)(128)(2,1)S(1)} %dynamic-slice.6, bf16[112]{0:T(256)(128)(2,1)S(1)} %dynamic-slice.8), channel_id=1, replica_groups=mesh['ctx'=16,'wa'=8] {'ctx'}, use_global_device_ids=true, to_apply=%region_22.23 | all-reduce | flops 368 | bytes 1472 | tf_op jit(solution)/shard_map/psum | solution.py:380
  692.2 0.9 fusion.35
  693.1 45.8 %all-reduce.14.cloned.1.call-done = (bf16[112,1152]{1,0:T(8,128)(2,1)}, bf16[112,896]{1,0:T(8,128)(2,1)}, bf16[112,9728]{1,0:T(8,128)(2,1)}, bf16[608,896]{1,0:T(8,128)(2,1)}) async-done(((bf16[112,1152]{1,0:T(8,128)(2,1)}, bf16[112,896]{1,0:T(8,128)(2,1)}, bf16[112,9728]{1,0:T(8,128)(2,1)}, bf16[608,896]{1,0:T(8,128)(2,1)}), (bf16[112,1152]{1,0:T(8,128)(2,1)}, bf16[112,896]{1,0:T(8,128)(2,1)}, ...) | async-done | bytes 3727376 | tf_op jit(solution)/shard_map/psum | solution.py:381
  738.9 1.8 convert_element_type.194
  740.7 1.8 convert_element_type.197
  742.5 4.1 convert_element_type.201
  746.6 1.5 convert_element_type.203
  (148 shorter events, 22.1 us)
Async XLA Ops:
  7.2 2.9 copy-start.14
  7.2 4.8 copy-start.15
  7.2 5.0 copy-start.16
  7.2 5.3 copy-start.17
  7.2 20.3 %copy-start.4 = (bf16[1,128,896]{2,1,0:T(8,128)(2,1)S(1)}, bf16[1,128,896]{2,1,0:T(8,128)(2,1)}, u32[]{:S(2)}) copy-start(bf16[1,128,896]{2,1,0:T(8,128)(2,1)} %param.22) | copy-start | bytes 688132
  7.2 20.4 %copy-start.13 = (s32[1,128]{1,0:T(1,128)S(1)}, s32[1,128]{1,0:T(1,128)}, u32[]{:S(2)}) copy-start(s32[1,128]{1,0:T(1,128)} %param.23) | copy-start | bytes 1540
  7.2 31.5 %all-gather.5.cloned.1.call-start = ((), (), s32[]{:S(2)}) async-start(), calls=%async_computation.6 | async-start | bytes 2322432 | tf_op jit(solution)/shard_map/all_gather | solution.py:225
  8.0 85.8 %all-gather.7.cloned.1.call-start = ((), (), s32[]{:S(2)}) async-start(), calls=%async_computation.7 | async-start | bytes 1806336 | tf_op jit(solution)/shard_map/all_gather | solution.py:227
  8.7 146.2 %all-gather.9.cloned.1.call-start = ((), (), s32[]{:S(2)}) async-start(), calls=%async_computation.8 | async-start | bytes 19611648 | tf_op jit(solution)/shard_map/all_gather | solution.py:229
  9.5 198.8 %all-gather.11.cloned.1.call-start = ((), (), s32[]{:S(2)}) async-start(), calls=%async_computation.9 | async-start | bytes 9805824 | tf_op jit(solution)/shard_map/all_gather | solution.py:230
  10.0 326.6 %reduce-scatter.21.cloned.1.call-start = ((), (), s32[]{:S(2)}) async-start(), calls=%async_computation.15 | async-start | bytes 557056
  93.7 0.8 copy-start.3
  93.7 72.3 %copy-start.6 = (f32[128,2,7,64]{0,3,2,1:T(8,128)}, f32[128,2,7,64]{0,3,2,1:T(8,128)S(1)}, u32[]{:S(2)}) copy-start(f32[128,2,7,64]{0,3,2,1:T(8,128)S(1)} %get-tuple-element.626) | copy-start | bytes 1376260
  93.8 72.3 %copy-start.9 = (bf16[128,2,7,64]{0,3,2,1:T(8,128)(2,1)}, bf16[128,2,7,64]{0,3,2,1:T(8,128)(2,1)S(1)}, u32[]{:S(2)}) copy-start(bf16[128,2,7,64]{0,3,2,1:T(8,128)(2,1)S(1)} %convert_element_type.178) | copy-start | bytes 688132
  217.2 13.9 %copy-start = (f32[128,4864]{1,0:T(8,128)}, f32[128,4864]{1,0:T(8,128)S(1)}, u32[]{:S(2)}) copy-start(f32[128,4864]{1,0:T(8,128)S(1)} %get-tuple-element.777) | copy-start | bytes 7471108
  231.1 4.3 copy-start.7
  232.4 0.8 copy-start.1
  237.2 15.2 %copy-start.10 = (bf16[128,2,7,64]{0,3,2,1:T(8,128)(2,1)S(1)}, bf16[128,2,7,64]{0,3,2,1:T(8,128)(2,1)}, u32[]{:S(2)}) copy-start(bf16[128,2,7,64]{0,3,2,1:T(8,128)(2,1)} %copy-done.9) | copy-start | bytes 688132
  249.9 161.6 %reduce-scatter.19.cloned.1.call-start = ((), (), s32[]{:S(2)}) async-start(), calls=%async_computation.14 | async-start | bytes 557056
  252.3 160.2 %copy-start.5 = (bf16[1,128,896]{2,1,0:T(8,128)(2,1)S(1)}, bf16[1,128,896]{2,1,0:T(8,128)(2,1)}, u32[]{:S(2)}) copy-start(bf16[1,128,896]{2,1,0:T(8,128)(2,1)} %param.22) | copy-start | bytes 688132
  252.3 192.7 %reduce-scatter.13.cloned.1.call-start = ((), (), s32[]{:S(2)}) async-start(), calls=%async_computation.11 | async-start | bytes 1806336 | tf_op jit(solution)/shard_map/reduce_scatter | solution.py:366
  255.2 159.5 %copy-start.12 = (bf16[1,128,896]{2,1,0:T(8,128)(2,1)S(1)}, bf16[1,128,896]{2,1,0:T(8,128)(2,1)}, u32[]{:S(2)}) copy-start(bf16[1,128,896]{2,1,0:T(8,128)(2,1)} %param.31) | copy-start | bytes 688132
  255.2 225.2 %reduce-scatter.11.cloned.1.call-start = ((), (), s32[]{:S(2)}) async-start(), calls=%async_computation.10 | async-start | bytes 2322432 | tf_op jit(solution)/shard_map/reduce_scatter | solution.py:360
  414.6 123.5 %reduce-scatter.17.cloned.1.call-start = ((), (), s32[]{:S(2)}) async-start(), calls=%async_computation.13 | async-start | bytes 9805824 | tf_op jit(solution)/shard_map/reduce_scatter | solution.py:375
  419.4 215.8 %reduce-scatter.15.cloned.1.call-start = ((), (), s32[]{:S(2)}) async-start(), calls=%async_computation.12 | async-start | bytes 19611648 | tf_op jit(solution)/shard_map/reduce_scatter | solution.py:372
  429.8 309.2 %all-reduce.14.cloned.1.call-start = ((), (), s32[]{:S(2)}) async-start(), calls=%async_computation.16 | async-start | bytes 7454720 | tf_op jit(solution)/shard_map/psum | solution.py:381
  636.5 6.0 copy-start.8
  642.3 49.9 %copy-start.2 = (f32[128,896]{1,0:T(8,128)S(1)}, f32[128,896]{1,0:T(8,128)}, u32[]{:S(2)}) copy-start(f32[128,896]{1,0:T(8,128)} %copy-done.1) | copy-start | bytes 1376260
  740.7 5.9 copy-start.11
Sparse Core Ops, SparseCore 0:
  9.8 28.9 all-gather.4
  40.4 24.7 all-gather.6
  66.9 87.9 all-gather.8
  156.5 51.7 all-gather.10
  250.1 86.5 reduce-scatter.20
  340.0 71.4 reduce-scatter.18
  413.9 31.0 reduce-scatter.12
  448.0 32.3 reduce-scatter.10
  482.8 55.2 reduce-scatter.16
  540.6 94.4 reduce-scatter.14
  639.0 99.9 all-reduce.13
where the time goes:
time: 755 us
  waiting for transfers between devices  521 us (69%)
  blocking collectives  99.9 us (13%)
  matrix products  72.5 us (10%)
  local copies, waits for them, and re-layouts  20.1 us (3%)
  between operations  17 us (2%)
  other arithmetic  15.1 us (2%)
  loops' own time  8.62 us (1%)
    unnamed x13, waiting for transfers between devices  158 us
    reduce_scatter x1, waiting for transfers between devices, on_device(): lax.psum_scatter(local_all[5].astype(jnp.bfloat16), 'wa', scatter_dimensi...  97 us
    all_gather x1, waiting for transfers between devices, on_device(): lax.all_gather(shards[5], 'wa', axis=0, tiled=True)  58.3 us
    reduce_scatter x1, waiting for transfers between devices, on_device(): lax.psum_scatter(local_all[6].astype(jnp.bfloat16), 'wa', scatter_dimensi...  57.8 us
    psum x1, waiting for transfers between devices, on_device(): lax.psum(rows_all[1].astype(jnp.bfloat16), 'ctx').astype(jnp.float32)  45.8 us
    all_gather x1, waiting for transfers between devices, on_device(): lax.all_gather(shards[6], 'wa', axis=0, tiled=True)  42.3 us
    reduce_scatter x1, waiting for transfers between devices, on_device(): lax.psum_scatter(local_all[1].astype(jnp.bfloat16), 'wa', scatter_dimensi...  35.4 us
    psum x1, blocking collectives, on_device(): lax.psum(rows_all[0].astype(jnp.bfloat16), 'ctx').astype(jnp.float32)  33.2 us
  transfers between devices with their start and end apart: 11, of which 10 were waited for; matrix products, arithmetic and copies ran while one was open for 8% of the time, Pallas kernels for 0%

commit v1 on v0

--- a/solution.py
+++ b/solution.py
@@ -199,6 +199,55 @@
     return lax.fori_loop(0, length // token_block, visit, start_state)
 
 
+def core_swap(value):
+    return lax.ppermute(value, "wa", [(i, i ^ 1) for i in range(8)])
+
+
+Z_GROUPS = [[0, 2, 4, 6], [1, 3, 5, 7]]
+
+
+def z_exchange(value):
+    return lax.all_to_all(value, "wa", 0, 0, tiled=True, axis_index_groups=Z_GROUPS)
+
+
+def z_gather(value):
+    return z_exchange(jnp.broadcast_to(value[None], (4,) + value.shape))
+
+
+def ctx_exchange(value):
+    return lax.all_to_all(value, "ctx", 0, 0, tiled=True)
+
+
+def core_order(own, other, core, axis):
+    first = jnp.where(core == 0, own, other)
+    second = jnp.where(core == 0, other, own)
+    return jnp.stack([first, second], axis=axis)
+
+
+def gather_rows(value, core):
+    own = z_gather(value)
+    return core_order(own, core_swap(own), core, 1).reshape((8,) + value.shape)
+
+
+def gather_tokens(value):
+    own = z_gather(value)
+    return jnp.concatenate([own, core_swap(own)], axis=0)
+
+
+def reduce_tokens(partial):
+    sent = core_swap(partial[4:].astype(jnp.bfloat16))
+    mine = (partial[:4] + sent.astype(jnp.float32)).astype(jnp.bfloat16)
+    return jnp.sum(z_exchange(mine).astype(jnp.float32), axis=0)
+
+
+def reduce_rows(partial, core):
+    pairs = partial.reshape((4, 2) + partial.shape[1:])
+    kept = jnp.where(core == 0, pairs[:, 0], pairs[:, 1])
+    sent = jnp.where(core == 0, pairs[:, 1], pairs[:, 0])
+    mine = (kept.astype(jnp.float32) + core_swap(sent).astype(jnp.float32)).astype(jnp.bfloat16)
+    return jnp.sum(z_exchange(mine).astype(jnp.float32), axis=0)
+
+
 def on_device(
     layer_input,
     positions,
@@ -211,97 +260,117 @@
     down_matrix,
     cotangent,
 ):
-    shards = (
-        attention_gain,
-        projection,
-        projection_biases,
-        output_matrix,
-        feed_gain,
-        gate_up_matrix,
-        down_matrix,
-    )
-    gain_one, full_proj, full_bias, complete_output, gain_two, full_gate_up, full_down = (
-        lax.all_gather(shards[0], "wa", axis=0, tiled=True),
-        lax.all_gather(shards[1], "wa", axis=0, tiled=True),
-        lax.all_gather(shards[2], "wa", axis=0, tiled=True),
-        lax.all_gather(shards[3], "wa", axis=0, tiled=True),
-        lax.all_gather(shards[4], "wa", axis=0, tiled=True),
-        lax.all_gather(shards[5], "wa", axis=0, tiled=True),
-        lax.all_gather(shards[6], "wa", axis=0, tiled=True),
-    )
-    block_count = layer_input.shape[1]
+    core = lax.axis_index("wa") % 2
+    rows = projection.shape[0]
+    tokens = layer_input.shape[1]
     head_group = QUERY_HEADS // KEY_VALUE_HEADS
-    query_total_width = QUERY_HEADS * HEAD_SIZE
-    key_total_width = KEY_VALUE_HEADS * HEAD_SIZE
+    query_width = QUERY_HEADS * HEAD_SIZE
+    key_width = KEY_VALUE_HEADS * HEAD_SIZE
+    width = layer_input.shape[2]
+    proj_width = projection.shape[1]
+    bias_rows = projection_biases.shape[0]
+    slice_width = down_matrix.shape[0]
+    lanes = -(-slice_width // 128) * 128
+    pad_rows = 16
+
+    small = jnp.concatenate([projection_biases, attention_gain, feed_gain])
+    small = jnp.pad(small[None], ((0, pad_rows - 1), (0, proj_width - small.shape[0])))
+    packed = gather_rows(jnp.concatenate([projection, small], axis=0), core)
+    full_proj = packed[:, :rows].reshape(width, proj_width)
+    vectors = packed[:, rows].astype(jnp.float32)
+    full_bias = vectors[:, :bias_rows].reshape(proj_width)
+    gain_one = vectors[:, bias_rows : bias_rows + rows].reshape(width)
+    gain_two = vectors[:, bias_rows + rows : bias_rows + 2 * rows].reshape(width)
+    complete_output = lax.all_gather(output_matrix, "wa", axis=0, tiled=True)
+
+    by_core = gate_up_matrix.reshape(rows, 2, 4, 2, slice_width)
+    kept = jnp.where(core == 0, by_core[:, :, :, 0], by_core[:, :, :, 1])
+    sent = jnp.where(core == 0, by_core[:, :, :, 1], by_core[:, :, :, 0])
+    widen = ((0, 0), (0, 0), (0, 0), (0, lanes - slice_width))
+    kept = jnp.pad(kept, widen).transpose(2, 0, 1, 3).reshape(4, rows, 2 * lanes)
+    sent = jnp.pad(sent, widen).transpose(2, 0, 1, 3).reshape(4, rows, 2 * lanes)
+    gate_up = z_exchange(core_order(kept, core_swap(sent), core, 1).reshape(4, 2 * rows, 2 * lanes))
+    gate_up = gate_up.reshape(width, 2 * lanes)
+    down = jnp.pad(down_matrix, ((0, lanes - slice_width), (0, 0)))
+
+    out_grad = cotangent[0]
+    all_out_grad = gather_tokens(out_grad).reshape(8 * tokens, width)
+
     decoder_layer = layer_input[0].astype(jnp.float32)
     query_pos = positions[0]
-    query_index = lax.axis_index("ctx") * block_count + jnp.arange(block_count, dtype=jnp.int32)
-    first_normed = norm_rows(decoder_layer, gain_one.astype(jnp.float32)).astype(jnp.bfloat16)
-    projected_rows = jnp.dot(
-        first_normed, full_proj, preferred_element_type=jnp.float32
-    ) + full_bias.astype(jnp.float32)
+    query_index = lax.axis_index("ctx") * tokens + jnp.arange(tokens, dtype=jnp.int32)
+    first_normed = norm_rows(decoder_layer, gain_one).astype(jnp.bfloat16)
+    projected_rows = jnp.dot(first_normed, full_proj, preferred_element_type=jnp.float32) + full_bias
     cosine_table, sine_table = angles(query_pos)
     cosine_table = cosine_table[:, None, :]
     sine_table = sine_table[:, None, :]
     query_rows = rotate(
-        projected_rows[:, :query_total_width].reshape(block_count, QUERY_HEADS, HEAD_SIZE),
+        projected_rows[:, :query_width].reshape(tokens, QUERY_HEADS, HEAD_SIZE),
         cosine_table,
         sine_table,
     ).astype(jnp.bfloat16)
     key_rows = rotate(
-        projected_rows[:, query_total_width : query_total_width + key_total_width].reshape(
-            block_count, KEY_VALUE_HEADS, HEAD_SIZE
+        projected_rows[:, query_width : query_width + key_width].reshape(
+            tokens, KEY_VALUE_HEADS, HEAD_SIZE
         ),
         cosine_table,
         sine_table,
     )
-    key_rows = key_rows.astype(jnp.bfloat16).reshape(block_count, key_total_width)
-    value_rows = projected_rows[:, query_total_width + key_total_width :].astype(jnp.bfloat16)
-    all_keys, all_values = (
-        lax.all_gather(key_rows, "ctx", axis=0, tiled=True),
-        lax.all_gather(value_rows, "ctx", axis=0, tiled=True),
-    )
+    key_rows = key_rows.astype(jnp.bfloat16).reshape(tokens, key_width)
+    value_rows = projected_rows[:, query_width + key_width :].astype(jnp.bfloat16)
+    pair = jnp.concatenate([key_rows, value_rows], axis=1)
+    pairs = ctx_exchange(jnp.broadcast_to(pair[None], (16,) + pair.shape))
+    pairs = pairs.reshape(16 * tokens, 2 * key_width)
+    all_keys, all_values = pairs[:, :key_width], pairs[:, key_width:]
     token_block = math.gcd(512, all_keys.shape[0])
-    grouped_queries = query_rows.reshape(block_count, KEY_VALUE_HEADS, head_group, HEAD_SIZE)
+    grouped_queries = query_rows.reshape(tokens, KEY_VALUE_HEADS, head_group, HEAD_SIZE)
     peak, total = key_stats(grouped_queries, all_keys, query_index, query_pos, token_block)
     mixed = key_mix(
         grouped_queries, all_keys, all_values, query_index, query_pos, peak, total, token_block
     )
-    attention_output = mixed.reshape(block_count, query_total_width).astype(jnp.bfloat16)
+    attention_output = mixed.reshape(tokens, query_width).astype(jnp.bfloat16)
     middle_state = decoder_layer + jnp.dot(
         attention_output, complete_output, preferred_element_type=jnp.float32
     )
-    second_normed = norm_rows(middle_state, gain_two.astype(jnp.float32)).astype(jnp.bfloat16)
-    joined_heads = jnp.dot(second_normed, full_gate_up, preferred_element_type=jnp.float32)
-    hidden_f, swiglu_pull = jax.vjp(swiglu, joined_heads)
-    hidden_state = hidden_f.astype(jnp.bfloat16)
-    result = (
-        middle_state + jnp.dot(hidden_state, full_down, preferred_element_type=jnp.float32)
-    ).astype(jnp.bfloat16)
-    gain_one, full_proj, full_bias, complete_output, gain_two, full_gate_up, full_down = (
-        lax.all_gather(shards[0], "wa", axis=0, tiled=True),
-        lax.all_gather(shards[1], "wa", axis=0, tiled=True),
-        lax.all_gather(shards[2], "wa", axis=0, tiled=True),
-        lax.all_gather(shards[3], "wa", axis=0, tiled=True),
-        lax.all_gather(shards[4], "wa", axis=0, tiled=True),
-        lax.all_gather(shards[5], "wa", axis=0, tiled=True),
-        lax.all_gather(shards[6], "wa", axis=0, tiled=True),
-    )
-    out_grad = cotangent[0]
-    down_local = rows_product(hidden_state, out_grad)
-    hidden_grad = column_product(out_grad, full_down)
-    joined_grad = swiglu_pull(hidden_grad)[0].astype(jnp.bfloat16)
-    gate_up_local = rows_product(second_normed, joined_grad)
-    normed_two_grad = column_product(joined_grad, full_gate_up)
-    _, norm_two_pull = jax.vjp(norm_rows, middle_state, gain_two.astype(jnp.float32))
+    second_normed = norm_rows(middle_state, gain_two).astype(jnp.bfloat16)
+
+    all_normed = gather_tokens(second_normed).reshape(8 * tokens, width)
+    joined = jnp.dot(all_normed, gate_up, preferred_element_type=jnp.float32)
+    gate, up = joined[:, :lanes], joined[:, lanes:]
+    hidden_grad = column_product(all_out_grad, down)
+    sg = jax.nn.sigmoid(gate)
+    act = gate * sg
+    hidden_state = (act * up).astype(jnp.bfloat16)
+    gate_grad = hidden_grad * up * sg * (1.0 + gate * (1.0 - sg))
+    up_grad = hidden_grad * act
+    joined_grad = jnp.concatenate([gate_grad, up_grad], axis=1).astype(jnp.bfloat16)
+    normed_two_grad = reduce_tokens(column_product(joined_grad, gate_up).reshape(8, tokens, width))
+    feed_out = reduce_tokens(
+        jnp.dot(hidden_state, down, preferred_element_type=jnp.float32).reshape(8, tokens, width)
+    )
+    result = (middle_state + feed_out).astype(jnp.bfloat16)
+    down_local = rows_product(hidden_state, all_out_grad)[:slice_width].astype(jnp.bfloat16)
+    gate_up_local = rows_product(all_normed, joined_grad).astype(jnp.bfloat16)
+    by_rows = gate_up_local.reshape(4, 2, rows, 2 * lanes)
+    kept = jnp.where(core == 0, by_rows[:, 0], by_rows[:, 1])
+    sent = jnp.where(core == 0, by_rows[:, 1], by_rows[:, 0])
+    gate_up_rows = z_exchange(
+        core_order(kept, core_swap(sent), core, 1).reshape(4, 2 * rows, 2 * lanes)
+    )
+    gate_up_rows = gate_up_rows.reshape(4, 2, rows, 2, lanes)[..., :slice_width]
+    gate_up_rows = gate_up_rows.transpose(2, 3, 0, 1, 4).reshape(rows, 16 * slice_width)
+    gate_up_total, down_total = lax.psum((gate_up_rows, down_local), "ctx")
+
+    _, norm_two_pull = jax.vjp(norm_rows, middle_state, gain_two)
     middle_part, gain_two_local = norm_two_pull(normed_two_grad)
     middle_grad = out_grad.astype(jnp.float32) + middle_part
     middle_lower = middle_grad.astype(jnp.bfloat16)
-    out_weight_local = rows_product(attention_output, middle_lower)
+    out_weight_local = rows_product(attention_output, middle_lower).astype(jnp.bfloat16)
+    out_weight_rows = lax.psum_scatter(out_weight_local, "wa", scatter_dimension=0, tiled=True)
     mix_grad = (
         column_product(middle_lower, complete_output)
         .astype(jnp.bfloat16)
-        .reshape(block_count, KEY_VALUE_HEADS, head_group, HEAD_SIZE)
+        .reshape(tokens, KEY_VALUE_HEADS, head_group, HEAD_SIZE)
     )
     delta = jnp.einsum("tkgd,tkgd->kgt", mix_grad.astype(jnp.float32), mixed)
     query_grad, key_grad, value_grad = key_grads(
@@ -316,85 +385,61 @@
         total,
         token_block,
     )
-    local_key_rows, own_values = (
-        lax.psum_scatter(
-            key_grad.astype(jnp.bfloat16), "ctx", scatter_dimension=0, tiled=True
-        ).astype(jnp.float32),
-        lax.psum_scatter(
-            value_grad.astype(jnp.bfloat16), "ctx", scatter_dimension=0, tiled=True
-        ).astype(jnp.float32),
+    pair_grad = jnp.concatenate([key_grad, value_grad], axis=1).astype(jnp.bfloat16)
+    pair_grad = jnp.sum(
+        ctx_exchange(pair_grad.reshape(16, tokens, 2 * key_width)).astype(jnp.float32), axis=0
     )
     score_scale = HEAD_SIZE ** (-0.5)
     query_back = inverse_rotate(
-        (query_grad * score_scale).reshape(block_count, QUERY_HEADS, HEAD_SIZE),
+        (query_grad * score_scale).reshape(tokens, QUERY_HEADS, HEAD_SIZE),
         cosine_table,
         sine_table,
-    ).reshape(block_count, query_total_width)
+    ).reshape(tokens, query_width)
     key_restored = inverse_rotate(
-        (local_key_rows * score_scale).reshape(block_count, KEY_VALUE_HEADS, HEAD_SIZE),
+        (pair_grad[:, :key_width] * score_scale).reshape(tokens, KEY_VALUE_HEADS, HEAD_SIZE),
         cosine_table,
         sine_table,
-    ).reshape(block_count, key_total_width)
-    projected_grad = jnp.concatenate([query_back, key_restored, own_values], axis=1).astype(
-        jnp.bfloat16
-    )
-    proj_local = rows_product(first_normed, projected_grad)
+    ).reshape(tokens, key_width)
+    projected_grad = jnp.concatenate(
+        [query_back, key_restored, pair_grad[:, key_width:]], axis=1
+    ).astype(jnp.bfloat16)
+    proj_local = rows_product(first_normed, projected_grad).astype(jnp.bfloat16)
     bias_local = jnp.sum(projected_grad.astype(jnp.float32), axis=0)
     normed_one_grad = column_product(projected_grad, full_proj)
-    _, norm_one_pull = jax.vjp(norm_rows, decoder_layer, gain_one.astype(jnp.float32))
+    _, norm_one_pull = jax.vjp(norm_rows, decoder_layer, gain_one)
     layer_part, gain_one_local = norm_one_pull(normed_one_grad)
     input_grad = middle_grad + layer_part
-    local_all = (
-        gain_one_local,
-        proj_local,
-        bias_local,
-        out_weight_local,
-        gain_two_local,
-        gate_up_local,
-        down_local,
-    )
-    rows_all = (
-        lax.psum_scatter(
-            local_all[0].astype(jnp.bfloat16), "wa", scatter_dimension=0, tiled=True
-        ).astype(jnp.float32),
-        lax.psum_scatter(
-            local_all[1].astype(jnp.bfloat16), "wa", scatter_dimension=0, tiled=True
-        ).astype(jnp.float32),
-        lax.psum_scatter(
-            local_all[2].astype(jnp.bfloat16), "wa", scatter_dimension=0, tiled=True
-        ).astype(jnp.float32),
-        lax.psum_scatter(
-            local_all[3].astype(jnp.bfloat16), "wa", scatter_dimension=0, tiled=True
-        ).astype(jnp.float32),
-        lax.psum_scatter(
-            local_all[4].astype(jnp.bfloat16), "wa", scatter_dimension=0, tiled=True
-        ).astype(jnp.float32),
-        lax.psum_scatter(
-            local_all[5].astype(jnp.bfloat16), "wa", scatter_dimension=0, tiled=True
-        ).astype(jnp.float32),
-        lax.psum_scatter(
-            local_all[6].astype(jnp.bfloat16), "wa", scatter_dimension=0, tiled=True
-        ).astype(jnp.float32),
-    )
-    totals = (
-        lax.psum(rows_all[0].astype(jnp.bfloat16), "ctx").astype(jnp.float32),
-        lax.psum(rows_all[1].astype(jnp.bfloat16), "ctx").astype(jnp.float32),
-        lax.psum(rows_all[2].astype(jnp.bfloat16), "ctx").astype(jnp.float32),
-        lax.psum(rows_all[3].astype(jnp.bfloat16), "ctx").astype(jnp.float32),
-        lax.psum(rows_all[4].astype(jnp.bfloat16), "ctx").astype(jnp.float32),
-        lax.psum(rows_all[5].astype(jnp.bfloat16), "ctx").astype(jnp.float32),
-        lax.psum(rows_all[6].astype(jnp.bfloat16), "ctx").astype(jnp.float32),
-    )
+
+    small = jnp.concatenate(
+        [
+            bias_local.reshape(8, bias_rows),
+            gain_one_local.reshape(8, rows),
+            gain_two_local.reshape(8, rows),
+        ],
+        axis=1,
+    ).astype(jnp.bfloat16)
+    small = jnp.pad(small[:, None], ((0, 0), (0, pad_rows - 1), (0, proj_width - small.shape[1])))
+    mine = reduce_rows(
+        jnp.concatenate([proj_local.reshape(8, rows, proj_width), small], axis=1), core
+    ).astype(jnp.bfloat16)
+    out_weight_rows = jnp.pad(out_weight_rows, ((0, pad_rows), (0, 0)))
+    mine = jnp.concatenate([mine, out_weight_rows], axis=1)
+    columns = mine.shape[1] // 16
+    mine = mine.reshape(rows + pad_rows, 16, columns).transpose(1, 0, 2)
+    mine = jnp.sum(ctx_exchange(mine).astype(jnp.float32), axis=0).astype(jnp.bfloat16)
+    mine = ctx_exchange(jnp.broadcast_to(mine[None], (16,) + mine.shape))
+    mine = mine.transpose(1, 0, 2).reshape(rows + pad_rows, 16 * columns).astype(jnp.float32)
+    vectors = mine[rows]
     return (
         result[None],
         input_grad[None],
-        totals[0],
-        totals[1],
-        totals[2],
-        totals[3],
-        totals[4],
-        totals[5],
-        totals[6],
+        vectors[bias_rows : bias_rows + rows],
+        mine[:rows, :proj_width],
+        vectors[:bias_rows],
+        mine[:rows, proj_width:],
+        vectors[bias_rows + rows : bias_rows + 2 * rows],
+        gate_up_total.astype(jnp.float32),
+        down_total.astype(jnp.float32),
     )
 
 

time: 755 us -> 437 us (0.58); the launches traced: 755 us -> 428 us
  waiting for transfers between devices: 521 us -> 141 us
  starting transfers between devices: 0.66 us -> 84.7 us
  blocking collectives: 99.9 us -> 31.1 us
  local copies, waits for them, and re-layouts: 20.1 us -> 70.5 us
  matrix products: 72.5 us -> 30.6 us
  other arithmetic: 15.1 us -> 46.7 us
    reduce_scatter x4 -> x1, waiting for transfers between devices: 205 us -> 0.02 us  [on_device(): lax.psum_scatter(out_weight_local, 'wa', scatter_dimension=0, tiled=True)]
    unnamed x13 -> x3, waiting for transfers between devices: 158 us -> 0.74 us
    all_gather x4 -> x1, waiting for transfers between devices: 112 us -> 0.01 us  [on_device(): complete_output = lax.all_gather(output_matrix, 'wa', axis=0, tiled=True)]
    all_to_all x0 -> x10, waiting for transfers between devices: none -> 93.3 us  [the longest x7 65 us: z_exchange(): lax.all_to_all(value, 'wa', 0, 0, tiled=True, axis_index_groups=Z_GROUPS)]
    all_to_all x0 -> x10, starting transfers between devices: none -> 69.8 us  [the longest x3 38.2 us: ctx_exchange(): return lax.all_to_all(value, 'ctx', 0, 0, tiled=True)]
    all_gather x2 -> x0, blocking collectives: 38.2 us -> none  [the longest x1 19.7 us: on_device(): lax.all_gather(value_rows, 'ctx', axis=0, tiled=True)]
    psum x1 -> x0, blocking collectives: 33.2 us -> none  [on_device(): lax.psum(rows_all[0].astype(jnp.bfloat16), 'ctx').astype(jnp.float32)]
    all_to_all x0 -> x2, blocking collectives: none -> 31.1 us  [the longest x1 16.1 us: z_exchange(): lax.all_to_all(value, 'wa', 0, 0, tiled=True, axis_index_groups=Z_GROUPS)]
  transfers between devices with their start and end apart: 11 -> 21, of which waited for: 10 -> 11; matrix products, arithmetic and copies ran while one was open for 8% -> 24% of each run, Pallas kernels for 0% -> 0%
where the time goes in v1:
time: 437 us; the launch traced here: 428 us
  waiting for transfers between devices  141 us (32%)
  starting transfers between devices  84.7 us (19%)
  local copies, waits for them, and re-layouts  70.5 us (16%)
  other arithmetic  46.7 us (11%)
  blocking collectives  31.1 us (7%)
  matrix products  30.6 us (7%)
  between operations  15.1 us (3%)
  loops' own time  8.47 us (2%)
    all_to_all x7, waiting for transfers between devices, z_exchange(): lax.all_to_all(value, 'wa', 0, 0, tiled=True, axis_index_groups=Z_GROUPS)  65 us
    psum x1, waiting for transfers between devices, on_device(): gate_up_total, down_total = lax.psum((gate_up_rows, down_local), 'ctx')  45 us
    all_to_all x3, starting transfers between devices, ctx_exchange(): return lax.all_to_all(value, 'ctx', 0, 0, tiled=True)  38.2 us
    all_to_all x7, starting transfers between devices, z_exchange(): lax.all_to_all(value, 'wa', 0, 0, tiled=True, axis_index_groups=Z_GROUPS)  31.7 us
    all_to_all x3, waiting for transfers between devices, ctx_exchange(): return lax.all_to_all(value, 'ctx', 0, 0, tiled=True)  28.3 us
    all_to_all x1, blocking collectives, z_exchange(): lax.all_to_all(value, 'wa', 0, 0, tiled=True, axis_index_groups=Z_GROUPS)  16.1 us
    all_to_all x1, blocking collectives, ctx_exchange(): return lax.all_to_all(value, 'ctx', 0, 0, tiled=True)  15 us
    ppermute x8, starting transfers between devices, core_swap(): return lax.ppermute(value, 'wa', [(i, i ^ 1) for i in range(8)])  14.8 us
  transfers between devices with their start and end apart: 21, of which 11 were waited for; matrix products, arithmetic and copies ran while one was open for 24% of the time, Pallas kernels for 0%

profile of v1, /device:TPU:1, one launch (start us, length us, event | category | flops | bytes accessed | tf_op | source)
XLA Modules:
  0.0 428.3 jit_solution(12798460460144965575)
XLA Ops:
  10.0 5.9 %all-to-all-start = ((bf16[4,128,1152]{2,1,0:T(8,128)(2,1)}), bf16[4,128,1152]{2,1,0:T(8,128)(2,1)}, u32[]{:S(2)}, u32[]{:S(2)}) async-start(bf16[4,128,1152]{2,1,0:T(8,128)(2,1)} %broadcast_in_dim.104), calls=%async_computation | async-start | bytes 2359296 | tf_op jit(solution)/shard_map/all_to_all | solution.py:210
  16.6 7.3 %reshape.362 = bf16[112,2,4,2,608]{4,3,2,1,0:T(2,128)(2,1)S(1)} reshape(bf16[112,9728]{1,0:T(8,128)(2,1)} %param.29) | data formatting | bytes 4358144 | tf_op jit(solution)/shard_map/reshape | solution.py:286
  24.3 7.2 %all-to-all-done = bf16[4,128,1152]{2,1,0:T(8,128)(2,1)} async-done(((bf16[4,128,1152]{2,1,0:T(8,128)(2,1)}), bf16[4,128,1152]{2,1,0:T(8,128)(2,1)}, u32[]{:S(2)}, u32[]{:S(2)}) %all-to-all-start) | async-done | bytes 1179680 | tf_op jit(solution)/shard_map/all_to_all | solution.py:210
  33.4 6.4 %broadcast_select_fusion.1 = (bf16[112,2,4,1,608]{4,3,2,1,0:T(2,128)(2,1)}, bf16[112,2,4,1,608]{4,3,2,1,0:T(2,128)(2,1)}) fusion(pred[]{:T(512)S(6)} %eq.4, bf16[112,2,4,2,608]{4,3,2,1,0:T(2,128)(2,1)S(1)} %reshape.362), kind=kLoop, calls=%fused_computation.48 | loop fusion | flops 1089536 | bytes 4358145 | tf_op jit(solution)/shard_map/jit(_where)/select_n | solution.py:287
  46.0 6.8 %all-to-all-start.1 = ((bf16[16,128,256]{1,2,0:T(8,128)(2,1)}), bf16[16,128,256]{1,2,0:T(8,128)(2,1)}, u32[]{:S(2)}, u32[]{:S(2)}) async-start(bf16[16,128,256]{1,2,0:T(8,128)(2,1)} %broadcast_in_dim.105), calls=%async_computation.1 | async-start | bytes 2097152 | tf_op jit(solution)/shard_map/all_to_all | solution.py:218
  52.8 3.4 copy_bitcast_fusion
  59.9 9.8 %all-to-all-done.1 = bf16[16,128,256]{1,2,0:T(8,128)(2,1)} async-done(((bf16[16,128,256]{1,2,0:T(8,128)(2,1)}), bf16[16,128,256]{1,2,0:T(8,128)(2,1)}, u32[]{:S(2)}, u32[]{:S(2)}) %all-to-all-start.1) | async-done | bytes 1048608 | tf_op jit(solution)/shard_map/all_to_all | solution.py:218
  70.8 4.4 %all-to-all-start.5 = ((bf16[4,128,896]{2,1,0:T(8,128)(2,1)}), bf16[4,128,896]{2,1,0:T(8,128)(2,1)}, u32[]{:S(2)}, u32[]{:S(2)}) async-start(bf16[4,128,896]{2,1,0:T(8,128)(2,1)} %broadcast_in_dim.110), calls=%async_computation.5 | async-start | bytes 1835008 | tf_op jit(solution)/shard_map/all_to_all | solution.py:210
  75.2 2.3 copy.203
  79.2 6.9 %while.48 = (s32[]{:T(128)}, f32[2,7,128]{2,1,0:T(8,128)S(1)}, f32[2,7,128]{2,1,0:T(8,128)S(1)}, s32[128]{0:T(128)S(1)}, s32[1,128]{1,0:T(1,128)S(1)}, /*index=5...) while((s32[]{:T(128)}, f32[2,7,128]{2,1,0:T(8,128)S(1)}, ...), condition=%wide.region_6.7_spmd, body=%wide.region_1.6_spmd.sunk | while | flops 125046784 | bytes 8257809 | solution.py:102
  86.2 6.7 %while.49 = (s32[]{:T(128)}, f32[128,2,7,64]{0,3,2,1:T(8,128)S(1)}, s32[128]{0:T(128)S(1)}, bf16[2048,128]{0,1:T(8,128)(2,1)S(1)}, s32[1,128]{1,0:T(1,128)S(1)},...) while((s32[]{:T(128)}, f32[128,2,7,64]{0,3,2,1:T(8,128)S(1)}, ...), condition=%wide.region_10.11_spmd, body=%wide.region_7.10_spmd.sunk | while | flops 240763392 | bytes 2084113 | solution.py:136
  97.0 4.2 all-to-all-start.2
  104.5 7.8 %all-to-all-done.2 = bf16[4,128,896]{2,1,0:T(8,128)(2,1)} async-done(((bf16[4,128,896]{2,1,0:T(8,128)(2,1)}), bf16[4,128,896]{2,1,0:T(8,128)(2,1)}, u32[]{:S(2)}, u32[]{:S(2)}) %all-to-all-start.2) | async-done | bytes 917536 | tf_op jit(solution)/shard_map/all_to_all | solution.py:210
  112.3 3.6 all-to-all-start.3
  115.9 3.8 collective-permute-start.4
  122.0 2.6 pad_maximum_fusion.5
  124.7 2.6 pad_maximum_fusion.4
  127.3 13.4 %all-to-all-done.3 = bf16[4,224,1280]{2,1,0:T(8,128)(2,1)S(1)} async-done(((bf16[4,224,1280]{2,1,0:T(8,128)(2,1)}), bf16[4,224,1280]{2,1,0:T(8,128)(2,1)S(1)}, u32[]{:S(2)}, u32[]{:S(2)}) %all-to-all-start.3) | async-done | bytes 2293792 | tf_op jit(solution)/shard_map/all_to_all | solution.py:210
  140.7 4.5 %fusion.83 = f32[1024,1280]{1,0:T(8,128)S(1)} fusion(bf16[1024,896]{1,0:T(8,128)(2,1)} %bitcast.310, bf16[896,1280]{1,0:T(8,128)(2,1)S(1)} %bitcast.298), kind=kOutput, calls=%fused_computation.197 | convolution fusion | flops 2348810240 | bytes 9371648 | tf_op jit(solution)/shard_map/dot_general | solution.py:338
  145.2 2.5 multiply_convert_fusion.1
  147.8 2.9 fusion.26
  150.7 2.6 convolution_convert_fusion
  153.4 4.7 %collective-permute-start.5 = (bf16[4,128,896]{2,1,0:T(8,128)(2,1)S(1)}, bf16[4,128,896]{2,1,0:T(8,128)(2,1)S(1)}, u32[]{:S(2)}, u32[]{:S(2)}) collective-permute-start(bf16[4,128,896]{2,1,0:T(8,128)(2,1)S(1)} %bitcast.314), channel_id=1, source_target_pairs={{0,1},{1,0},{2,3},{3,2},{4,5},{5,4},{6,7},{7,6},{8,9},{9,8},{10,11... | collective-permute-start | bytes 2752520 | tf_op jit(solution)/shard_map/ppermute | solution.py:203
  165.7 4.2 all-to-all-start.6
  171.4 2.4 add_convert_fusion.1
  173.8 10.0 %all-to-all-done.6 = bf16[4,128,896]{2,1,0:T(8,128)(2,1)} async-done(((bf16[4,128,896]{2,1,0:T(8,128)(2,1)}), bf16[4,128,896]{2,1,0:T(8,128)(2,1)}, u32[]{:S(2)}, u32[]{:S(2)}) %all-to-all-start.6) | async-done | bytes 917536 | tf_op jit(solution)/shard_map/all_to_all | solution.py:210
  183.8 4.7 %all-to-all-start.4 = ((bf16[4,128,896]{2,1,0:T(8,128)(2,1)}), bf16[4,128,896]{2,1,0:T(8,128)(2,1)}, u32[]{:S(2)}, u32[]{:S(2)}) async-start(bf16[4,128,896]{2,1,0:T(8,128)(2,1)} %add_convert_fusion.1), calls=%async_computation.4 | async-start | bytes 1835008 | tf_op jit(solution)/shard_map/all_to_all | solution.py:210
  188.5 2.9 fusion.27
  193.6 7.9 %all-to-all-done.4 = bf16[4,128,896]{2,1,0:T(8,128)(2,1)} async-done(((bf16[4,128,896]{2,1,0:T(8,128)(2,1)}), bf16[4,128,896]{2,1,0:T(8,128)(2,1)}, u32[]{:S(2)}, u32[]{:S(2)}) %all-to-all-start.4) | async-done | bytes 917536 | tf_op jit(solution)/shard_map/all_to_all | solution.py:210
  203.7 2.2 convolution_convert_fusion.3
  206.3 10.0 %while.50 = (s32[]{:T(128)}, f32[128,2,7,64]{0,3,2,1:T(8,128)S(1)}, bf16[2048,128]{0,1:T(8,128)(2,1)S(1)}, bf16[2048,128]{0,1:T(8,128)(2,1)S(1)}, s32[128]{0:T(1...) while((s32[]{:T(128)}, f32[128,2,7,64]{0,3,2,1:T(8,128)S(1)}, ...), condition=%wide.region_18.19_spmd, body=%wide.region_15.18_spmd.sunk | while | flops 595837440 | bytes 20212104 | solution.py:199
  207.6 4.9 %conditional.8 = ((f32[128,2,7,64]{0,3,2,1:T(8,128)S(1)}, bf16[2048,128]{0,1:T(8,128)(2,1)S(1)}, bf16[2048,128]{0,1:T(8,128)(2,1)S(1)})) conditional(s32[]{:T(128)} %convert_element_type.331, (f32[128,2,7,64]{0,3,2,1:T(8,128)S(1)}, bf16[2048,128]{0,1:T(8,128)(2,1)S(1)}, bf16[2048,128]{0,1:T(8,128)(2,1)S(1)}) %tuple.148, (s32[]{:T(128)}, ...), branch_computations={%region_16.16_spmd, %region_17.17_spmd} | conditional | flops 595837440 | bytes 20211794 | solution.py:192
  218.1 2.4 copy.220
  220.4 27.8 %all-to-all-start.7 = ((bf16[16,128,256]{1,2,0:T(8,128)(2,1)}), bf16[16,128,256]{1,2,0:T(8,128)(2,1)}, u32[]{:S(2)}, u32[]{:S(2)}) async-start(bf16[16,128,256]{1,2,0:T(8,128)(2,1)} %copy.220), calls=%async_computation.7 | async-start | bytes 2097152 | tf_op jit(solution)/shard_map/all_to_all | solution.py:218
  253.3 9.8 %all-to-all-done.7 = bf16[16,128,256]{1,2,0:T(8,128)(2,1)} async-done(((bf16[16,128,256]{1,2,0:T(8,128)(2,1)}), bf16[16,128,256]{1,2,0:T(8,128)(2,1)}, u32[]{:S(2)}, u32[]{:S(2)}) %all-to-all-start.7) | async-done | bytes 1048608 | tf_op jit(solution)/shard_map/all_to_all | solution.py:218
  263.2 4.6 %all-to-all-start.11 = ((bf16[4,224,1280]{2,1,0:T(8,128)(2,1)}), bf16[4,224,1280]{2,1,0:T(8,128)(2,1)}, u32[]{:S(2)}, u32[]{:S(2)}) async-start(bf16[4,224,1280]{2,1,0:T(8,128)(2,1)} %bitcast.93), calls=%async_computation.12 | async-start | bytes 4587520 | tf_op jit(solution)/shard_map/all_to_all | solution.py:210
  275.2 3.3 collective-permute-start.6
  281.2 18.6 %all-to-all-done.11 = bf16[4,224,1280]{2,1,0:T(8,128)(2,1)} async-done(((bf16[4,224,1280]{2,1,0:T(8,128)(2,1)}), bf16[4,224,1280]{2,1,0:T(8,128)(2,1)}, u32[]{:S(2)}, u32[]{:S(2)}) %all-to-all-start.11) | async-done | bytes 2293792 | tf_op jit(solution)/shard_map/all_to_all | solution.py:210
  299.8 5.5 %reshape.376 = bf16[4,2,112,2,640]{4,3,2,1,0:T(2,128)(2,1)} reshape(bf16[4,224,1280]{2,1,0:T(8,128)(2,1)} %all-to-all-done.11) | data formatting | bytes 4587520 | tf_op jit(solution)/shard_map/reshape | solution.py:360
  305.3 3.2 slice_bitcast_fusion
  308.6 3.2 copy.229
  311.8 6.3 %reshape.377 = bf16[112,9728]{1,0:T(8,128)(2,1)} reshape(bf16[112,2,4,2,608]{4,3,2,1,0:T(2,128)(2,1)} %copy.229) | data formatting | bytes 4358144 | tf_op jit(solution)/shard_map/reshape | solution.py:361
  319.9 16.1 %all_to_all.60 = bf16[4,128,1152]{2,1,0:T(8,128)(2,1)S(1)} all-to-all(bf16[4,128,1152]{2,1,0:T(8,128)(2,1)S(1)} %fusion.25), channel_id=1, replica_groups={{0,2,4,6},{1,3,5,7},{8,10,12,14},{9,11,13,15},{16,18,20,22},{17,19,21,2..., dimensions={0} | all-to-all | bytes 2359296 | tf_op jit(solution)/shard_map/all_to_all | solution.py:210
  337.8 15.0 %all_to_all.61 = bf16[16,128,128]{2,1,0:T(8,128)(2,1)S(1)} all-to-all(bf16[16,128,128]{2,1,0:T(8,128)(2,1)S(1)} %copy.224), channel_id=1, replica_groups=mesh['ctx'=16,'wa'=8] {'ctx'}, dimensions={0} | all-to-all | bytes 1048576 | tf_op jit(solution)/shard_map/all_to_all | solution.py:218
  353.7 3.6 all-to-all-start.10
  358.3 8.7 %all-to-all-done.10 = bf16[16,128,128]{2,1,0:T(8,128)(2,1)S(1)} async-done(((bf16[16,128,128]{2,1,0:T(8,128)(2,1)}), bf16[16,128,128]{2,1,0:T(8,128)(2,1)S(1)}, u32[]{:S(2)}, u32[]{:S(2)}) %all-to-all-start.10) | async-done | bytes 524320 | tf_op jit(solution)/shard_map/all_to_all | solution.py:218
  370.8 45.0 %all-reduce.9.cloned.1.call-done = (bf16[112,9728]{1,0:T(8,128)(2,1)}, bf16[608,896]{1,0:T(8,128)(2,1)}) async-done(((bf16[112,9728]{1,0:T(8,128)(2,1)}, bf16[608,896]{1,0:T(8,128)(2,1)}), (bf16[112,9728]{1,0:T(8,128)(2,1)}, bf16[608,896]{1,0:T(8,128)(2,1)})) %all-reduce.9.cloned.1.call-update) | async-done | bytes 3268624 | tf_op jit(solution)/shard_map/psum | solution.py:362
  415.9 4.2 convert_element_type.239
  (276 shorter events, 87.6 us)
Async XLA Ops:
  10.0 21.6 %all-to-all-start = ((bf16[4,128,1152]{2,1,0:T(8,128)(2,1)}), bf16[4,128,1152]{2,1,0:T(8,128)(2,1)}, u32[]{:S(2)}, u32[]{:S(2)}) async-start(bf16[4,128,1152]{2,1,0:T(8,128)(2,1)} %broadcast_in_dim.104), calls=%async_computation | async-start | bytes 2359296 | tf_op jit(solution)/shard_map/all_to_all | solution.py:210
  15.9 77.8 %all-gather.2.cloned.1.call-start = ((), (), s32[]{:S(2)}) async-start(), calls=%async_computation.13 | async-start | bytes 1806336 | tf_op jit(solution)/shard_map/all_gather | solution.py:284
  16.6 7.4 %copy-start.7 = (bf16[1,128,896]{2,1,0:T(8,128)(2,1)S(1)}, bf16[1,128,896]{2,1,0:T(8,128)(2,1)}, u32[]{:S(2)}) copy-start(bf16[1,128,896]{2,1,0:T(8,128)(2,1)} %param.22) | copy-start | bytes 688132
  16.6 7.5 %copy-start.23 = (s32[1,128]{1,0:T(1,128)S(1)}, s32[1,128]{1,0:T(1,128)}, u32[]{:S(2)}) copy-start(s32[1,128]{1,0:T(1,128)} %param.23) | copy-start | bytes 1540
  24.1 15.7 %copy-start.39 = (f32[128]{0:T(128)}, f32[128]{0:T(128)S(1)}, u32[]{:S(2)}) copy-start(f32[128]{0:T(128)S(1)} %fusion.48) | copy-start | bytes 1540
  24.2 17.9 %copy-start.34 = (f32[128]{0:T(128)}, f32[128]{0:T(128)S(1)}, u32[]{:S(2)}) copy-start(f32[128]{0:T(128)S(1)} %fusion.72) | copy-start | bytes 1540
  31.6 8.3 %collective-permute-start = (bf16[4,128,1152]{2,1,0:T(8,128)(2,1)}, bf16[4,128,1152]{2,1,0:T(8,128)(2,1)S(1)}, u32[]{:S(2)}, u32[]{:S(2)}) collective-permute-start(bf16[4,128,1152]{2,1,0:T(8,128)(2,1)} %all-to-all-done), channel_id=1, source_target_pairs={{0,1},{1,0},{2,3},{3,2},{4,5},{5,4},{6,7},{7,6},{8,9},{9,8},{10,11... | collective-permute-start | bytes 3538952 | tf_op jit(solution)/shard_map/ppermute | solution.py:203
  43.6 9.2 %copy-start = (bf16[112,2,4,1,608]{4,3,2,1,0:T(2,128)(2,1)S(1)}, bf16[112,2,4,1,608]{4,3,2,1,0:T(2,128)(2,1)}, u32[]{:S(2)}) copy-start(bf16[112,2,4,1,608]{4,3,2,1,0:T(2,128)(2,1)} %get-tuple-element.856) | copy-start | bytes 3268612
  46.0 23.7 %all-to-all-start.1 = ((bf16[16,128,256]{1,2,0:T(8,128)(2,1)}), bf16[16,128,256]{1,2,0:T(8,128)(2,1)}, u32[]{:S(2)}, u32[]{:S(2)}) async-start(bf16[16,128,256]{1,2,0:T(8,128)(2,1)} %broadcast_in_dim.105), calls=%async_computation.1 | async-start | bytes 2097152 | tf_op jit(solution)/shard_map/all_to_all | solution.py:218
  57.5 43.8 %collective-permute-start.2 = (bf16[4,112,1280]{2,1,0:T(8,128)(2,1)}, bf16[4,112,1280]{2,1,0:T(8,128)(2,1)}, u32[]{:S(2)}, u32[]{:S(2)}) collective-permute-start(bf16[4,112,1280]{2,1,0:T(8,128)(2,1)} %bitcast.117), channel_id=1, source_target_pairs={{0,1},{1,0},{2,3},{3,2},{4,5},{5,4},{6,7},{7,6},{8,9},{9,8},{10,11... | collective-permute-start | bytes 3440648 | tf_op jit(solution)/shard_map/ppermute | solution.py:203
  58.0 11.7 %copy-start.20 = (bf16[1,128,896]{2,1,0:T(8,128)(2,1)S(1)}, bf16[1,128,896]{2,1,0:T(8,128)(2,1)}, u32[]{:S(2)}) copy-start(bf16[1,128,896]{2,1,0:T(8,128)(2,1)} %param.31) | copy-start | bytes 688132
  70.8 25.3 %all-to-all-start.5 = ((bf16[4,128,896]{2,1,0:T(8,128)(2,1)}), bf16[4,128,896]{2,1,0:T(8,128)(2,1)}, u32[]{:S(2)}, u32[]{:S(2)}) async-start(bf16[4,128,896]{2,1,0:T(8,128)(2,1)} %broadcast_in_dim.110), calls=%async_computation.5 | async-start | bytes 1835008 | tf_op jit(solution)/shard_map/all_to_all | solution.py:210
  86.1 7.6 %copy-start.8 = (bf16[1,128,896]{2,1,0:T(8,128)(2,1)S(1)}, bf16[1,128,896]{2,1,0:T(8,128)(2,1)}, u32[]{:S(2)}) copy-start(bf16[1,128,896]{2,1,0:T(8,128)(2,1)} %param.22) | copy-start | bytes 688132
  95.8 6.8 %copy-start.41 = (f32[128]{0:T(128)}, f32[128]{0:T(128)S(1)}, u32[]{:S(2)}) copy-start(f32[128]{0:T(128)S(1)} %get-tuple-element.874) | copy-start | bytes 1540
  95.9 6.8 %copy-start.36 = (f32[128]{0:T(128)}, f32[128]{0:T(128)S(1)}, u32[]{:S(2)}) copy-start(f32[128]{0:T(128)S(1)} %fusion.73) | copy-start | bytes 1540
  97.0 15.3 %all-to-all-start.2 = ((bf16[4,128,896]{2,1,0:T(8,128)(2,1)}), bf16[4,128,896]{2,1,0:T(8,128)(2,1)}, u32[]{:S(2)}, u32[]{:S(2)}) async-start(bf16[4,128,896]{2,1,0:T(8,128)(2,1)} %broadcast_in_dim.108), calls=%async_computation.2 | async-start | bytes 1835008 | tf_op jit(solution)/shard_map/all_to_all | solution.py:210
  112.3 28.4 %all-to-all-start.3 = ((bf16[4,224,1280]{2,1,0:T(8,128)(2,1)}), bf16[4,224,1280]{2,1,0:T(8,128)(2,1)S(1)}, u32[]{:S(2)}, u32[]{:S(2)}) async-start(bf16[4,224,1280]{2,1,0:T(8,128)(2,1)} %bitcast.61), calls=%async_computation.3 | async-start | bytes 4587520 | tf_op jit(solution)/shard_map/all_to_all | solution.py:210
  115.9 6.1 %collective-permute-start.4 = (bf16[4,128,896]{2,1,0:T(8,128)(2,1)}, bf16[4,128,896]{2,1,0:T(8,128)(2,1)S(1)}, u32[]{:S(2)}, u32[]{:S(2)}) collective-permute-start(bf16[4,128,896]{2,1,0:T(8,128)(2,1)} %all-to-all-done.5), channel_id=1, source_target_pairs={{0,1},{1,0},{2,3},{3,2},{4,5},{5,4},{6,7},{7,6},{8,9},{9,8},{10,11... | collective-permute-start | bytes 2752520 | tf_op jit(solution)/shard_map/ppermute | solution.py:203
  119.7 4.9 %collective-permute-start.1 = (bf16[4,128,896]{2,1,0:T(8,128)(2,1)}, bf16[4,128,896]{2,1,0:T(8,128)(2,1)S(1)}, u32[]{:S(2)}, u32[]{:S(2)}) collective-permute-start(bf16[4,128,896]{2,1,0:T(8,128)(2,1)} %all-to-all-done.2), channel_id=1, source_target_pairs={{0,1},{1,0},{2,3},{3,2},{4,5},{5,4},{6,7},{7,6},{8,9},{9,8},{10,11... | collective-permute-start | bytes 2752520 | tf_op jit(solution)/shard_map/ppermute | solution.py:203
  140.7 4.5 %copy-start.16 = (bf16[8,128,896]{2,1,0:T(8,128)(2,1)S(1)}, bf16[8,128,896]{2,1,0:T(8,128)(2,1)}, u32[]{:S(2)}) copy-start(bf16[8,128,896]{2,1,0:T(8,128)(2,1)} %pad_maximum_fusion.5) | copy-start | bytes 5505028
  140.7 4.5 %copy-start.43 = (bf16[608,896]{1,0:T(8,128)(2,1)S(1)}, bf16[608,896]{1,0:T(8,128)(2,1)}, u32[]{:S(2)}) copy-start(bf16[608,896]{1,0:T(8,128)(2,1)} %param.30) | copy-start | bytes 3268612
  147.8 10.3 %copy-start.44 = (bf16[1024,640]{1,0:T(8,128)(2,1)}, bf16[1024,640]{1,0:T(8,128)(2,1)S(1)}, u32[]{:S(2)}) copy-start(bf16[1024,640]{1,0:T(8,128)(2,1)S(1)} %get-tuple-element.849) | copy-start | bytes 3932164
  153.4 11.1 %collective-permute-start.5 = (bf16[4,128,896]{2,1,0:T(8,128)(2,1)S(1)}, bf16[4,128,896]{2,1,0:T(8,128)(2,1)S(1)}, u32[]{:S(2)}, u32[]{:S(2)}) collective-permute-start(bf16[4,128,896]{2,1,0:T(8,128)(2,1)S(1)} %bitcast.314), channel_id=1, source_target_pairs={{0,1},{1,0},{2,3},{3,2},{4,5},{5,4},{6,7},{7,6},{8,9},{9,8},{10,11... | collective-permute-start | bytes 2752520 | tf_op jit(solution)/shard_map/ppermute | solution.py:203
  162.7 7.1 %collective-permute-start.3 = (bf16[4,128,896]{2,1,0:T(8,128)(2,1)}, bf16[4,128,896]{2,1,0:T(8,128)(2,1)}, u32[]{:S(2)}, u32[]{:S(2)}) collective-permute-start(bf16[4,128,896]{2,1,0:T(8,128)(2,1)} %bitcast.64), channel_id=1, source_target_pairs={{0,1},{1,0},{2,3},{3,2},{4,5},{5,4},{6,7},{7,6},{8,9},{9,8},{10,11... | collective-permute-start | bytes 2752520 | tf_op jit(solution)/shard_map/ppermute | solution.py:203
  163.9 24.6 %collective-permute-start.7 = (bf16[4,112,1280]{2,1,0:T(8,128)(2,1)}, bf16[4,112,1280]{2,1,0:T(8,128)(2,1)}, u32[]{:S(2)}, u32[]{:S(2)}) collective-permute-start(bf16[4,112,1280]{2,1,0:T(8,128)(2,1)} %select_bitcast_fusion.3), channel_id=1, source_target_pairs={{0,1},{1,0},{2,3},{3,2},{4,5},{5,4},{6,7},{7,6},{8,9},{9,8},{10,11... | collective-permute-start | bytes 3440648 | tf_op jit(solution)/shard_map/ppermute | solution.py:203
  165.7 18.1 %all-to-all-start.6 = ((bf16[4,128,896]{2,1,0:T(8,128)(2,1)}), bf16[4,128,896]{2,1,0:T(8,128)(2,1)}, u32[]{:S(2)}, u32[]{:S(2)}) async-start(bf16[4,128,896]{2,1,0:T(8,128)(2,1)} %add_convert_fusion), calls=%async_computation.6 | async-start | bytes 1835008 | tf_op jit(solution)/shard_map/all_to_all | solution.py:210
  183.8 17.7 %all-to-all-start.4 = ((bf16[4,128,896]{2,1,0:T(8,128)(2,1)}), bf16[4,128,896]{2,1,0:T(8,128)(2,1)}, u32[]{:S(2)}, u32[]{:S(2)}) async-start(bf16[4,128,896]{2,1,0:T(8,128)(2,1)} %add_convert_fusion.1), calls=%async_computation.4 | async-start | bytes 1835008 | tf_op jit(solution)/shard_map/all_to_all | solution.py:210
  188.5 4.4 %copy-start.31 = (f32[896]{0:T(1024)S(1)}, f32[896]{0:T(1024)}, u32[]{:S(2)}) copy-start(f32[896]{0:T(1024)} %mul.363) | copy-start | bytes 10756
  188.5 4.4 %copy-start.37 = (f32[128]{0:T(128)S(1)}, f32[128]{0:T(128)}, u32[]{:S(2)}) copy-start(f32[128]{0:T(128)} %copy-done.36) | copy-start | bytes 1540
  191.4 11.4 %copy-start.21 = (bf16[1,128,896]{2,1,0:T(8,128)(2,1)S(1)}, bf16[1,128,896]{2,1,0:T(8,128)(2,1)}, u32[]{:S(2)}) copy-start(bf16[1,128,896]{2,1,0:T(8,128)(2,1)} %param.31) | copy-start | bytes 688132
  191.4 11.4 %copy-start.32 = (f32[896]{0:T(1024)S(1)}, f32[896]{0:T(1024)}, u32[]{:S(2)}) copy-start(f32[896]{0:T(1024)} %mul.363) | copy-start | bytes 10756
  191.4 11.5 %copy-start.38 = (f32[128]{0:T(128)S(1)}, f32[128]{0:T(128)}, u32[]{:S(2)}) copy-start(f32[128]{0:T(128)} %copy-done.36) | copy-start | bytes 1540
  203.7 47.6 %copy-start.4 = (f32[128,896]{1,0:T(8,128)}, f32[128,896]{1,0:T(8,128)S(1)}, u32[]{:S(2)}) copy-start(f32[128,896]{1,0:T(8,128)S(1)} %get-tuple-element.864) | copy-start | bytes 1376260
  218.1 30.2 %copy-start.11 = (bf16[4,1,112,1280]{3,2,0,1:T(8,128)(2,1)S(1)}, bf16[4,1,112,1280]{3,2,0,1:T(8,128)(2,1)}, u32[]{:S(2)}) copy-start(bf16[4,1,112,1280]{3,2,0,1:T(8,128)(2,1)} %get-tuple-element.850) | copy-start | bytes 3440644
  220.4 42.8 %all-to-all-start.7 = ((bf16[16,128,256]{1,2,0:T(8,128)(2,1)}), bf16[16,128,256]{1,2,0:T(8,128)(2,1)}, u32[]{:S(2)}, u32[]{:S(2)}) async-start(bf16[16,128,256]{1,2,0:T(8,128)(2,1)} %copy.220), calls=%async_computation.7 | async-start | bytes 2097152 | tf_op jit(solution)/shard_map/all_to_all | solution.py:218
  248.2 88.0 %reduce-scatter.2.cloned.1.call-start = ((), (), s32[]{:S(2)}) async-start(), calls=%async_computation.14 | async-start | bytes 1806336 | tf_op jit(solution)/shard_map/reduce_scatter | solution.py:369
  263.2 6.2 %copy-start.9 = (bf16[1,128,896]{2,1,0:T(8,128)(2,1)S(1)}, bf16[1,128,896]{2,1,0:T(8,128)(2,1)}, u32[]{:S(2)}) copy-start(bf16[1,128,896]{2,1,0:T(8,128)(2,1)} %param.22) | copy-start | bytes 688132
  263.2 6.2 %copy-start.29 = (f32[896]{0:T(1024)S(1)}, f32[896]{0:T(1024)}, u32[]{:S(2)}) copy-start(f32[896]{0:T(1024)} %copy-done.28) | copy-start | bytes 10756
  263.2 6.2 %copy-start.35 = (f32[128]{0:T(128)S(1)}, f32[128]{0:T(128)}, u32[]{:S(2)}) copy-start(f32[128]{0:T(128)} %copy-done.34) | copy-start | bytes 1540
  263.2 36.6 %all-to-all-start.11 = ((bf16[4,224,1280]{2,1,0:T(8,128)(2,1)}), bf16[4,224,1280]{2,1,0:T(8,128)(2,1)}, u32[]{:S(2)}, u32[]{:S(2)}) async-start(bf16[4,224,1280]{2,1,0:T(8,128)(2,1)} %bitcast.93), calls=%async_computation.12 | async-start | bytes 4587520 | tf_op jit(solution)/shard_map/all_to_all | solution.py:210
  267.8 148.0 %all-reduce.9.cloned.1.call-start = ((), (), s32[]{:S(2)}) async-start(), calls=%async_computation.15 | async-start | bytes 6537216 | tf_op jit(solution)/shard_map/psum | solution.py:362
  273.9 4.6 %copy-start.17 = (bf16[8,128,896]{2,1,0:T(8,128)(2,1)S(1)}, bf16[8,128,896]{2,1,0:T(8,128)(2,1)}, u32[]{:S(2)}) copy-start(bf16[8,128,896]{2,1,0:T(8,128)(2,1)} %pad_maximum_fusion.5) | copy-start | bytes 5505028
  273.9 4.6 %copy-start.45 = (bf16[1024,640]{1,0:T(8,128)(2,1)S(1)}, bf16[1024,640]{1,0:T(8,128)(2,1)}, u32[]{:S(2)}) copy-start(bf16[1024,640]{1,0:T(8,128)(2,1)} %copy-done.44) | copy-start | bytes 3932164
  275.2 42.9 %collective-permute-start.6 = (bf16[4,128,1152]{2,1,0:T(8,128)(2,1)}, bf16[4,128,1152]{2,1,0:T(8,128)(2,1)}, u32[]{:S(2)}, u32[]{:S(2)}) collective-permute-start(bf16[4,128,1152]{2,1,0:T(8,128)(2,1)} %select_bitcast_fusion), channel_id=1, source_target_pairs={{0,1},{1,0},{2,3},{3,2},{4,5},{5,4},{6,7},{7,6},{8,9},{9,8},{10,11... | collective-permute-start | bytes 3538952 | tf_op jit(solution)/shard_map/ppermute | solution.py:203
  337.4 19.8 %copy-start.40 = (f32[128]{0:T(128)S(1)}, f32[128]{0:T(128)}, u32[]{:S(2)}) copy-start(f32[128]{0:T(128)} %copy-done.39) | copy-start | bytes 1540
  337.4 19.9 %copy-start.5 = (f32[128,896]{1,0:T(8,128)S(1)}, f32[128,896]{1,0:T(8,128)}, u32[]{:S(2)}) copy-start(f32[128,896]{1,0:T(8,128)} %copy-done.4) | copy-start | bytes 1376260
  337.5 19.9 %copy-start.22 = (f32[128,896]{1,0:T(8,128)S(1)}, f32[128,896]{1,0:T(8,128)}, u32[]{:S(2)}) copy-start(f32[128,896]{1,0:T(8,128)} %get-tuple-element.876) | copy-start | bytes 1376260
  353.7 13.2 %all-to-all-start.10 = ((bf16[16,128,128]{2,1,0:T(8,128)(2,1)}), bf16[16,128,128]{2,1,0:T(8,128)(2,1)S(1)}, u32[]{:S(2)}, u32[]{:S(2)}) async-start(bf16[16,128,128]{2,1,0:T(8,128)(2,1)} %broadcast_in_dim.114), calls=%async_computation.11 | async-start | bytes 1048576 | tf_op jit(solution)/shard_map/all_to_all | solution.py:218
  (21 other events, 44.6 us)
Sparse Core Ops, SparseCore 0:
  18.4 27.1 all-gather.1
  253.2 35.4 reduce-scatter.1
  318.3 97.5 all-reduce.8
